TPU v7x, 512 devices: a whole 4x4x16 slice. The times are simulated.
512 devices in a mesh: tm: 32 (over z, x_hi), space: 16 (over y, x_lo, core).
Axes of the slice: x: 4 (x_hi: 2, x_lo: 2; x = x_hi * 2 + x_lo), y: 4, z: 16, core: 2. Of those that a mesh axis runs over, the one named last changes fastest.
Arguments:
- multiplier: bfloat16 [32, 1280, 2560], P('tm', 'space'), may hold values from -6 to 6
- increment: bfloat16 [32, 1280, 2560], P('tm', 'space'), may hold values from -6 to 6
- wind_east: bfloat16 [32, 1280, 2560], P('tm', 'space'), may hold values from -0.3984375 to 0.3984375
- wind_north: bfloat16 [32, 1280, 2560], P('tm', 'space'), may hold values from -0.3984375 to 0.3984375
- variances: bfloat16 [32, 1280, 2560], P('tm', None, 'space'), may hold values from 0.3 to 36, as said below
Outputs:
- multiplier_out: bfloat16 [32, 1280, 2560], P('tm', 'space')
- increment_out: bfloat16 [32, 1280, 2560], P('tm', 'space')
Inputs may be any that keep to these rules, and one draw needn't show every extreme that they name: `variances`: positive.
All inputs are finite; a program needn't handle non-finite values.
Results may differ from a plain program's by a relative error of at most 0.0055.
The roundings to bfloat16 on the way count: a program that leaves them out, or rounds other values in their place, can miss the bound.
Values may be sent and summed in bfloat16 or wider, within the bound.
A program may use at most 128 MiB of HBM per device.

v0:
```python
import functools
import math

import jax
import jax.numpy as jnp
import ml_dtypes
import numpy as np
from jax import lax
from jax.experimental import pallas as pl
from jax.experimental.pallas import tpu as pltpu
from jax.sharding import PartitionSpec as P

STEPS = 4
DIFFUSION = 0.2
MESH = pl.DeviceIdType.MESH

ROWS = 80
NLON = 2560
NLAT = 1280
SPACE = 16
OWN = NLON // SPACE
MAIN = 128
TAIL = OWN - MAIN
MSG = 112
TOP = 16
PADDED = ROWS + 32
CHUNK = 256
CHUNKS = NLON // CHUNK
F32 = jnp.float32
BF16 = jnp.bfloat16


def longitude_table():
    row = np.arange(NLON)[:, None]
    col = np.arange(NLON)[None, :]
    half = NLON // 2
    wave = np.where(col <= half, col, col - half)
    angle = (wave * row % NLON) * (2.0 * math.pi / NLON)
    scale = np.where((col == 0) | (col == half), math.sqrt(1.0 / NLON), math.sqrt(2.0 / NLON))
    return (np.where(col <= half, np.cos(angle), np.sin(angle)) * scale).astype(ml_dtypes.bfloat16)


def latitude_table():
    mode = np.arange(NLAT)[:, None]
    row = np.arange(NLAT)[None, :]
    angle = (mode * (2 * row + 1) % (4 * NLAT)) * (math.pi / (2.0 * NLAT))
    scale = np.where(mode == 0, math.sqrt(1.0 / NLAT), math.sqrt(2.0 / NLAT))
    return (np.cos(angle) * scale).astype(ml_dtypes.bfloat16)


def column_order():
    first = [OWN * d + np.arange(MAIN) for d in range(SPACE)]
    last = [OWN * d + MAIN + np.arange(TAIL) for d in range(SPACE)]
    return np.concatenate(first + last)


@functools.lru_cache(maxsize=1)
def tables():
    lon = longitude_table()
    lat = latitude_table()
    order = column_order()
    forward = lon[:, order].reshape(NLON, CHUNKS, CHUNK).transpose(1, 0, 2)
    inverse = lon.T[order, :].reshape(NLON, CHUNKS, CHUNK).transpose(1, 0, 2)
    return (
        np.ascontiguousarray(forward),
        np.ascontiguousarray(inverse),
        np.ascontiguousarray(lat.reshape(4, 320, NLAT)),
        np.ascontiguousarray(lat.T.reshape(4, 320, NLAT)),
    )


def lane_group(shape):
    return lax.broadcasted_iota(jnp.int32, shape, 1) // TAIL


def turned(x, shift):
    shift = shift % x.shape[1]
    return x if shift == 0 else pltpu.roll(x, shift, 1)


def packed_tail(groups, from_group):
    place = lane_group((16, 128))
    head = jnp.zeros((16, 128), F32)
    for g in range(4):
        head = jnp.where(place == g, turned(groups[g], TAIL * (g - from_group)), head)
    last = turned(groups[4], TAIL * (0 - from_group))
    return jnp.concatenate([head, last], axis=0).astype(BF16)


def kernel(
    windows,
    mult_h, inc_h, east_h, north_h, var_h, lonf_h, loni_h, lat_h, latt_h,
    out1_h, out2_h,
    mult_v, inc_v, east_v, north_v, var_v, lonf_v, loni_v, lat_v, latt_v,
    inc_r, inc_edge_s, inc_edge_r, edge_s, edge_r, adj_s, adj_r,
    state, half_e, half_n,
    send1, recv1, send2, recv2,
    cols, scaled, grid, varf, out1_v, out2_v,
    load_sem, lonf_sem, loni_sem, out_sem,
    inc_ss, inc_rs, iedge_ss, iedge_rs, edge_ss, edge_rs, adj_ss, adj_rs,
    a1_ss, a1_rs, a2_ss, a2_rs,
):
    tm = lax.axis_index("tm")
    me = lax.axis_index("space")
    after = lax.rem(tm + 1, windows)
    before = lax.rem(tm + windows - 1, windows)
    up = lax.rem(me + SPACE - 1, SPACE)
    down = lax.rem(me + 1, SPACE)
    core = lax.rem(me, 2)
    chip = me // 2
    sibling = me + 1 - 2 * core
    band = me // 4
    seat = lax.rem(me, 4)

    barrier = pltpu.get_barrier_semaphore()
    for o in range(1, SPACE):
        pl.semaphore_signal(
            barrier, inc=1, device_id=(tm, lax.rem(me + o, SPACE)), device_id_type=MESH
        )
    for window in (after, before):
        for space in (me, up, down):
            pl.semaphore_signal(barrier, inc=1, device_id=(window, space), device_id_type=MESH)

    def load(src, dst, sem):
        copy = pltpu.make_async_copy(src, dst, sem)
        copy.start()
        return copy

    loads = {
        name: load(src, dst, load_sem.at[n])
        for n, (name, src, dst) in enumerate(
            (
                ("mult", mult_h, mult_v),
                ("inc", inc_h, inc_v),
                ("east", east_h, east_v),
                ("north", north_h, north_v),
                ("var", var_h, var_v),
            )
        )
    }
    lonf_loads = [load(lonf_h.at[8 + t], lonf_v.at[8 + t], lonf_sem.at[8 + t]) for t in range(2)]
    for j in range(8):
        which = lax.rem(chip + 1 + j, 8)
        lonf_loads.append(load(lonf_h.at[which], lonf_v.at[j], lonf_sem.at[j]))
    lat_load = load(lat_h, lat_v, load_sem.at[5])
    latt_load = load(latt_h, latt_v, load_sem.at[6])
    loni_loads = [load(loni_h.at[n], loni_v.at[n], loni_sem.at[n]) for n in range(CHUNKS)]

    pl.semaphore_wait(barrier, 21)

    inc_copy = pltpu.make_async_remote_copy(
        src_ref=inc_h, dst_ref=inc_r, send_sem=inc_ss, recv_sem=inc_rs,
        device_id=(after, me), device_id_type=MESH,
    )
    inc_copy.start()

    def edges(ref):
        first = ref[0:16, :].astype(F32)[0:STEPS]
        last = ref[ROWS - 16 : ROWS, :].astype(F32)[16 - STEPS : 16]
        return first, last

    def folded(rows):
        return jnp.concatenate([rows[:, 640 * q : 640 * (q + 1)] for q in range(4)], axis=0)

    for name in ("mult", "inc", "east", "north"):
        loads[name].wait()
    parts = [edges(ref) for ref in (mult_v, east_v, north_v)]
    blank = jnp.zeros((16 - 3 * STEPS, NLON), F32)
    for side in range(2):
        edge_s[side] = jnp.concatenate([part[side] for part in parts] + [blank], axis=0).astype(BF16)
    own_edges = edges(inc_v)
    for side in range(2):
        inc_edge_s[side] = folded(own_edges[side]).astype(BF16)
    edge_copies = []
    for side, space in ((0, up), (1, down)):
        edge_copies.append(
            pltpu.make_async_remote_copy(
                src_ref=edge_s.at[side], dst_ref=edge_r.at[1 - side],
                send_sem=edge_ss.at[side], recv_sem=edge_rs.at[1 - side],
                device_id=(tm, space), device_id_type=MESH,
            )
        )
        edge_copies.append(
            pltpu.make_async_remote_copy(
                src_ref=inc_edge_s.at[side], dst_ref=inc_edge_r.at[1 - side],
                send_sem=iedge_ss.at[side], recv_sem=iedge_rs.at[1 - side],
                device_id=(after, space), device_id_type=MESH,
            )
        )
    for copy in edge_copies:
        copy.start()

    for t in range(2):
        lonf_loads[t].wait()
        product = jnp.dot(mult_v[...], lonf_v[8 + t], preferred_element_type=F32)
        for q in range(2):
            tile = product[:, 128 * q : 128 * (q + 1)]
            groups = [tile[16 * g : 16 * (g + 1)] for g in range(5)]
            for r in range(4):
                recv_slot = 4 * (2 * t + q) + r
                slot = 2 * lax.rem(recv_slot // 2 + 15 - chip, 8) + recv_slot % 2
                send1[slot, ROWS:MSG, :] = packed_tail(groups, r)

    def a1_copy(slot, owner):
        return pltpu.make_async_remote_copy(
            src_ref=send1.at[slot], dst_ref=recv1.at[me],
            send_sem=a1_ss.at[slot], recv_sem=a1_rs.at[me],
            device_id=(tm, owner), device_id_type=MESH,
        )

    def lon_step(j, _):
        which = lax.rem(chip + 1 + j, 8)
        pltpu.make_async_copy(lonf_h.at[which], lonf_v.at[j], lonf_sem.at[j]).wait()
        product = jnp.dot(mult_v[...], lonf_v[j], preferred_element_type=F32).astype(BF16)
        for c in range(2):
            send1[2 * j + c, 0:ROWS, :] = product[:, 128 * c : 128 * (c + 1)]

        @pl.when(j < 7)
        def _():
            for c in range(2):
                a1_copy(2 * j + c, 2 * which + c).start()

        return 0

    lax.fori_loop(0, 8, lon_step, 0)
    a1_copy(14 + 1 - core, sibling).start()
    recv1[me] = send1[14 + core]

    for ref, src in ((half_e, east_v), (half_n, north_v)):
        ref[TOP : TOP + ROWS, :] = src[...].astype(F32) * 0.5
    state[0, TOP : TOP + ROWS, :] = mult_v[...].astype(F32)
    for side in range(2):
        edge_copies[2 * side].wait_recv()
    gap = jnp.zeros((8 - STEPS, NLON), F32)

    def outside(side, rows):
        parts = [gap, rows] if side == 0 else [rows, gap]
        return jnp.concatenate(parts, axis=0)

    halo_at = (TOP - 8, TOP + ROWS)
    inside = (me > 0, me < SPACE - 1)
    for side in range(2):
        rows = edge_r[side].astype(F32)
        at = pl.ds(halo_at[side], 8)
        state[0, at, :] = jnp.where(inside[side], outside(side, rows[0:STEPS]), 0.0)
        half_e[at, :] = outside(side, rows[STEPS : 2 * STEPS]) * 0.5
        half_n[at, :] = outside(side, rows[2 * STEPS : 3 * STEPS]) * 0.5

    sublane = lax.broadcasted_iota(jnp.int32, (8, NLON), 0)

    def near(ref, r):
        return ref[pl.ds(r - 8, 8), :], ref[pl.ds(r, 8), :], ref[pl.ds(r + 8, 8), :]

    def row_above(before, x):
        return pltpu.roll(jnp.where(sublane == 7, before, x), 1, 0)

    def row_below(x, behind):
        return pltpu.roll(jnp.where(sublane == 0, behind, x), 7, 0)

    def forward_strip(src, r):
        before, x, behind = near(src, r)
        above = row_above(before, x)
        below = row_below(x, behind)
        east = pltpu.roll(x, NLON - 1, 1)
        west = pltpu.roll(x, 1, 1)
        return (
            DIFFUSION * ((x + (east + west)) + (above + below))
            + half_e[pl.ds(r, 8), :] * (west - east)
            + half_n[pl.ds(r, 8), :] * (above - below)
        )

    def adjoint_strip(src, r):
        before, y, behind = near(src, r)
        n_before, n, n_behind = near(half_n, r)
        fifth = DIFFUSION * y
        zonal = half_e[pl.ds(r, 8), :] * y
        merid = n * y
        north = row_above((DIFFUSION - n_before) * before, fifth - merid)
        south = row_below(fifth + merid, (DIFFUSION + n_behind) * behind)
        return (
            (fifth + (north + south))
            + (pltpu.roll(fifth - zonal, 1, 1) + pltpu.roll(fifth + zonal, NLON - 1, 1))
        )

    def steps(strip):
        for step in range(STEPS):
            src, dst = state.at[step % 2], state.at[(step + 1) % 2]
            whole = step < STEPS - 1

            def one(i, _):
                r = pl.multiple_of(8 * i + (TOP - 8 if whole else TOP), 8)
                dst[pl.ds(r, 8), :] = strip(src, r)
                return 0

            lax.fori_loop(0, ROWS // 8 + (2 if whole else 0), one, 0)
            if whole:
                for side in range(2):
                    at = pl.ds(halo_at[side], 8)
                    dst[at, :] = jnp.where(inside[side], dst[at, :], 0.0)

    for at in (TOP - 16, TOP + ROWS + 8):
        for ref in (state.at[0], state.at[1], half_n):
            ref[pl.ds(at, 8), :] = jnp.zeros((8, NLON), F32)
    steps(adjoint_strip)
    adj_s[...] = state[0, TOP : TOP + ROWS, :].astype(BF16)
    adj_copy = pltpu.make_async_remote_copy(
        src_ref=adj_s, dst_ref=adj_r, send_sem=adj_ss, recv_sem=adj_rs,
        device_id=(before, me), device_id_type=MESH,
    )
    adj_copy.start()

    loads["var"].wait()
    varf[:, 0:OWN] = var_v[...].astype(F32).T
    varf[:, OWN:CHUNK] = jnp.zeros((NLAT, CHUNK - OWN), F32)
    lat_load.wait()
    latt_load.wait()

    def gather(o, _):
        source = lax.rem(me + o, SPACE)

        @pl.when(o > 0)
        def _():
            pltpu.make_async_remote_copy(
                src_ref=send1.at[0], dst_ref=recv1.at[source],
                send_sem=a1_ss.at[0], recv_sem=a1_rs.at[source],
                device_id=(tm, source), device_id_type=MESH,
            ).wait_recv()

        at = pl.multiple_of(source * ROWS, 16)
        cols[pl.ds(at, ROWS), 0:MAIN] = recv1[source, 0:ROWS, :]
        tail = recv1[source, ROWS:MSG, :].astype(F32)
        for g in range(5):
            rows = turned(tail[0:16], -TAIL * g) if g < 4 else tail[16:32]
            cols[pl.ds(pl.multiple_of(at + 16 * g, 16), 16), MAIN:CHUNK] = rows.astype(BF16)
        return 0

    lax.fori_loop(0, SPACE, gather, 0)

    def lat_step(m, _):
        at = pl.ds(pl.multiple_of(m * 320, 320), 320)
        product = jnp.dot(lat_v[m], cols[...], preferred_element_type=F32)
        scaled[at, :] = (product * varf[at, :]).astype(BF16)
        return 0

    lax.fori_loop(0, 4, lat_step, 0)

    def a2_copy(slot, owner):
        return pltpu.make_async_remote_copy(
            src_ref=send2.at[slot], dst_ref=recv2.at[me],
            send_sem=a2_ss.at[slot], recv_sem=a2_rs.at[me],
            device_id=(tm, owner), device_id_type=MESH,
        )

    def back_step(j, _):
        q = lax.rem(band + 1 + j, 4)
        product = jnp.dot(latt_v[q], scaled[...], preferred_element_type=F32)
        for r in range(4):
            block = product[ROWS * r : ROWS * (r + 1)]
            tile = block[:, MAIN:CHUNK]
            send2[4 * j + r, 0:ROWS, :] = block[:, 0:MAIN].astype(BF16)
            send2[4 * j + r, ROWS:MSG, :] = packed_tail(
                [tile[16 * g : 16 * (g + 1)] for g in range(5)], 0
            )

        @pl.when(j < 3)
        def _():
            for r in range(4):
                a2_copy(4 * j + r, 4 * q + r).start()

        return 0

    lax.fori_loop(0, 4, back_step, 0)
    for o in range(1, 4):
        other = lax.rem(seat + o, 4)
        a2_copy(12 + other, 4 * band + other).start()
    recv2[me] = send2[12 + seat]

    inc_copy.wait_recv()
    for side in range(2):
        edge_copies[2 * side + 1].wait_recv()
    state[0, TOP : TOP + ROWS, :] = inc_r[...].astype(F32)
    for side in range(2):
        rows = inc_edge_r[side].astype(F32)
        rows = jnp.concatenate([rows[STEPS * q : STEPS * (q + 1)] for q in range(4)], axis=1)
        state[0, pl.ds(halo_at[side], 8), :] = jnp.where(inside[side], outside(side, rows), 0.0)
    steps(forward_strip)

    adj_copy.wait_recv()
    kept = jnp.where(tm < windows - 1, 1.0, 0.0)
    out2_v[...] = (mult_v[...].astype(F32) - kept * adj_r[...].astype(F32)).astype(BF16)
    out2_copy = load(out2_v, out2_h, out_sem.at[0])

    for source in range(SPACE):

        @pl.when(source != me)
        def _():
            pltpu.make_async_remote_copy(
                src_ref=send2.at[0], dst_ref=recv2.at[source],
                send_sem=a2_ss.at[0], recv_sem=a2_rs.at[source],
                device_id=(tm, me), device_id_type=MESH,
            ).wait_recv()

    place = lane_group((16, 128))
    for q in range(4):
        tails = []
        for r in range(4):
            source = 4 * q + r
            grid[:, MAIN * source : MAIN * (source + 1)] = recv2[source, 0:ROWS, :]
            tails.append(recv2[source, ROWS:MSG, :].astype(F32))
        for g in range(5):
            rows = jnp.zeros((16, 128), F32)
            for r in range(4):
                part = tails[r][0:16] if g < 4 else tails[r][16:32]
                rows = jnp.where(place == r, turned(part, TAIL * (r - g % 4)), rows)
            at = SPACE * MAIN + 128 * q
            grid[16 * g : 16 * (g + 1), at : at + 128] = rows.astype(BF16)

    taken = jnp.where(tm > 0, 1.0, 0.0)

    def out_step(n, _):
        pltpu.make_async_copy(loni_h.at[n], loni_v.at[n], loni_sem.at[n]).wait()
        at = pl.ds(pl.multiple_of(n * CHUNK, CHUNK), CHUNK)
        term = jnp.dot(grid[...], loni_v[n], preferred_element_type=F32)
        ahead = state[0, TOP : TOP + ROWS, at]
        out1_v[:, at] = (term + inc_v[:, at].astype(F32) - taken * ahead).astype(BF16)
        return 0

    lax.fori_loop(0, CHUNKS, out_step, 0)
    out1_copy = load(out1_v, out1_h, out_sem.at[1])

    inc_copy.wait_send()
    for copy in edge_copies:
        copy.wait_send()
    adj_copy.wait_send()

    def sent(slot, _):
        for src, dst, ss, rs in ((send1, recv1, a1_ss, a1_rs), (send2, recv2, a2_ss, a2_rs)):
            own = (14 + core) if ss is a1_ss else (12 + seat)

            @pl.when(slot != own)
            def _():
                pltpu.make_async_remote_copy(
                    src_ref=src.at[slot], dst_ref=dst.at[me],
                    send_sem=ss.at[slot], recv_sem=rs.at[me],
                    device_id=(tm, sibling), device_id_type=MESH,
                ).wait_send()

        return 0

    lax.fori_loop(0, SPACE, sent, 0)
    out2_copy.wait()
    out1_copy.wait()


def shards(windows, multiplier, increment, wind_east, wind_north, variances):
    lonf, loni, lat, latt = (jnp.asarray(table) for table in tables())
    block = (ROWS, NLON)
    wide = (PADDED, NLON)
    dma = pltpu.SemaphoreType.DMA
    vmem = pltpu.VMEM
    first, last = pl.pallas_call(
        functools.partial(kernel, windows),
        out_shape=(jax.ShapeDtypeStruct(block, BF16), jax.ShapeDtypeStruct(block, BF16)),
        in_specs=[pl.BlockSpec(memory_space=pl.ANY)] * 9,
        out_specs=(pl.BlockSpec(memory_space=pl.ANY),) * 2,
        scratch_shapes=[
            vmem(block, BF16), vmem(block, BF16), vmem(block, BF16), vmem(block, BF16),
            vmem((OWN, NLAT), BF16),
            vmem((CHUNKS, NLON, CHUNK), BF16), vmem((CHUNKS, NLON, CHUNK), BF16),
            vmem((4, 320, NLAT), BF16), vmem((4, 320, NLAT), BF16),
            vmem(block, BF16), vmem((2, 16, 640), BF16), vmem((2, 16, 640), BF16),
            vmem((2, 16, NLON), BF16), vmem((2, 16, NLON), BF16),
            vmem(block, BF16), vmem(block, BF16),
            vmem((2, *wide), F32), vmem(wide, F32), vmem(wide, F32),
            vmem((SPACE, MSG, 128), BF16), vmem((SPACE, MSG, 128), BF16),
            vmem((SPACE, MSG, 128), BF16), vmem((SPACE, MSG, 128), BF16),
            vmem((NLAT, CHUNK), BF16), vmem((NLAT, CHUNK), BF16), vmem(block, BF16),
            vmem((NLAT, CHUNK), F32), vmem(block, BF16), vmem(block, BF16),
            dma((7,)), dma((CHUNKS,)), dma((CHUNKS,)), dma((2,)),
            dma, dma, dma((2,)), dma((2,)), dma((2,)), dma((2,)), dma, dma,
            dma((SPACE,)), dma((SPACE,)), dma((SPACE,)), dma((SPACE,)),
        ],
        compiler_params=pltpu.CompilerParams(
            collective_id=0, has_side_effects=True, vmem_limit_bytes=60 * 2**20
        ),
        cost_estimate=pl.CostEstimate(
            flops=3_145_728_000, bytes_accessed=36_000_000, transcendentals=0
        ),
    )(
        multiplier[0], increment[0], wind_east[0], wind_north[0],
        jnp.swapaxes(variances[0], 0, 1), lonf, loni, lat, latt,
    )
    return first[None], last[None]


def solution(mesh):
    placed = P("tm", "space", None)
    return jax.shard_map(
        functools.partial(shards, mesh.shape["tm"]),
        mesh=mesh,
        in_specs=(placed, placed, placed, placed, P("tm", None, "space")),
        out_specs=(placed, placed),
        check_vma=False,
    )
```

profile of v0, /device:TPU:1, one launch (start us, length us, event | category | flops | bytes accessed | tf_op | source)
XLA Modules:
  0.0 62.1 jit_solution(8067128159376488837)
XLA Ops:
  0.6 57.9 %shard_map.104 = (bf16[80,2560]{1,0:T(8,128)(2,1)}, bf16[80,2560]{1,0:T(8,128)(2,1)}) custom-call(bf16[80,2560]{1,0:T(8,128)(2,1)} %bitcast.11, bf16[80,2560]{1,0:T(8,128)(2,1)} %bitcast.12, bf16[80,2560]{1,0:T(8,128)(2,1)} %bitcast.13, bf16[80,2560]{1,0:T(8,128)(2,1)} %bitcast.14, bf16[160,1280]{1,0:T(8,128)(2,1)} %bitcast.15, ...), custom_call_target="tpu_custom_call" | custom-call | flops 3145728000 | bytes 36000000 | tf_op jit(solution)/shard_map/pallas_call | solution.py:461
  58.5 1.8 %copy.13 = bf16[1,80,2560]{2,1,0:T(8,128)(2,1)} copy(bf16[1,80,2560]{2,1,0:T(8,128)(2,1)} %bitcast.10) | data formatting | bytes 819200
  60.3 1.8 %copy.14 = bf16[1,80,2560]{2,1,0:T(8,128)(2,1)} copy(bf16[1,80,2560]{2,1,0:T(8,128)(2,1)} %bitcast.9) | data formatting | bytes 819200
where the time goes:
time: 62.3 us; the launch traced here: 62.1 us
  Pallas kernels  57.9 us (93%)
  local copies, waits for them, and re-layouts  3.56 us (6%)
  between operations  0.64 us (1%)
    pallas_call x1, Pallas kernels, shards(): pl.pallas_call(functools.partial(kernel, windows), out_shape=(jax.ShapeDt...  57.9 us
    unnamed x2, local copies, waits for them, and re-layouts  3.56 us

commit v1 on v0

--- a/solution.py
+++ b/solution.py
@@ -26,6 +26,8 @@
 PADDED = ROWS + 32
 CHUNK = 256
 CHUNKS = NLON // CHUNK
+INC_CUT = 16
+ADJ_CUT = 64
 F32 = jnp.float32
 BF16 = jnp.bfloat16
 
@@ -93,11 +95,11 @@
     out1_h, out2_h,
     mult_v, inc_v, east_v, north_v, var_v, lonf_v, loni_v, lat_v, latt_v,
     inc_r, inc_edge_s, inc_edge_r, edge_s, edge_r, adj_s, adj_r,
-    state, half_e, half_n,
+    state, state_b, half_e, half_n,
     send1, recv1, send2, recv2,
-    cols, scaled, grid, varf, out1_v, out2_v,
-    load_sem, lonf_sem, loni_sem, out_sem,
-    inc_ss, inc_rs, iedge_ss, iedge_rs, edge_ss, edge_rs, adj_ss, adj_rs,
+    cols, scaled, grid, varf, out1_v,
+    load_sem, lonf_sem, loni_sem, out1_sem,
+    inc_sem, iedge_ss, iedge_rs, edge_ss, edge_rs, adj_sem,
     a1_ss, a1_rs, a2_ss, a2_rs,
 ):
     tm = lax.axis_index("tm")
@@ -134,7 +136,6 @@
                 ("inc", inc_h, inc_v),
                 ("east", east_h, east_v),
                 ("north", north_h, north_v),
-                ("var", var_h, var_v),
             )
         )
     }
@@ -142,17 +143,22 @@
     for j in range(8):
         which = lax.rem(chip + 1 + j, 8)
         lonf_loads.append(load(lonf_h.at[which], lonf_v.at[j], lonf_sem.at[j]))
-    lat_load = load(lat_h, lat_v, load_sem.at[5])
-    latt_load = load(latt_h, latt_v, load_sem.at[6])
-    loni_loads = [load(loni_h.at[n], loni_v.at[n], loni_sem.at[n]) for n in range(CHUNKS)]
 
     pl.semaphore_wait(barrier, 21)
 
-    inc_copy = pltpu.make_async_remote_copy(
-        src_ref=inc_h, dst_ref=inc_r, send_sem=inc_ss, recv_sem=inc_rs,
-        device_id=(after, me), device_id_type=MESH,
-    )
-    inc_copy.start()
+    def exchange(src, dst, sem, to, cut):
+        return [
+            pltpu.make_async_remote_copy(
+                src_ref=src.at[rows], dst_ref=dst.at[rows],
+                send_sem=sem.at[2 * n], recv_sem=sem.at[2 * n + 1],
+                device_id=(to, me), device_id_type=MESH,
+            )
+            for n, rows in enumerate((pl.ds(0, cut), pl.ds(cut, ROWS - cut)))
+        ]
+
+    inc_copies = exchange(inc_h, inc_r, inc_sem, after, INC_CUT)
+    adj_copies = exchange(adj_s, adj_r, adj_sem, before, ADJ_CUT)
+    has_next, has_previous = tm < windows - 1, tm > 0
 
     def edges(ref):
         first = ref[0:16, :].astype(F32)[0:STEPS]
@@ -187,8 +193,14 @@
                 device_id=(after, space), device_id_type=MESH,
             )
         )
-    for copy in edge_copies:
+    for copy in (edge_copies[0], edge_copies[2]):
         copy.start()
+
+    @pl.when(has_next)
+    def _():
+        for copy in (edge_copies[1], edge_copies[3]):
+            copy.start()
+
 
     for t in range(2):
         lonf_loads[t].wait()
@@ -223,12 +235,23 @@
         return 0
 
     lax.fori_loop(0, 8, lon_step, 0)
+    loads["var"] = load(var_h, var_v, load_sem.at[4])
+    lat_load = load(lat_h, lat_v, load_sem.at[5])
+    latt_load = load(latt_h, latt_v, load_sem.at[6])
+    for n in range(CHUNKS):
+        load(loni_h.at[n], loni_v.at[n], loni_sem.at[n])
     a1_copy(14 + 1 - core, sibling).start()
     recv1[me] = send1[14 + core]
 
+    @pl.when(has_next)
+    def _():
+        for copy in inc_copies:
+            copy.start()
+
+
     for ref, src in ((half_e, east_v), (half_n, north_v)):
         ref[TOP : TOP + ROWS, :] = src[...].astype(F32) * 0.5
-    state[0, TOP : TOP + ROWS, :] = mult_v[...].astype(F32)
+    state[TOP : TOP + ROWS, :] = mult_v[...].astype(F32)
     for side in range(2):
         edge_copies[2 * side].wait_recv()
     gap = jnp.zeros((8 - STEPS, NLON), F32)
@@ -242,14 +265,17 @@
     for side in range(2):
         rows = edge_r[side].astype(F32)
         at = pl.ds(halo_at[side], 8)
-        state[0, at, :] = jnp.where(inside[side], outside(side, rows[0:STEPS]), 0.0)
+        state[at, :] = jnp.where(inside[side], outside(side, rows[0:STEPS]), 0.0)
         half_e[at, :] = outside(side, rows[STEPS : 2 * STEPS]) * 0.5
         half_n[at, :] = outside(side, rows[2 * STEPS : 3 * STEPS]) * 0.5
 
-    sublane = lax.broadcasted_iota(jnp.int32, (8, NLON), 0)
-
-    def near(ref, r):
-        return ref[pl.ds(r - 8, 8), :], ref[pl.ds(r, 8), :], ref[pl.ds(r + 8, 8), :]
+    sublane = lax.broadcasted_iota(jnp.int32, (8, 128), 0)
+    lane = lax.broadcasted_iota(jnp.int32, (8, 128), 1)
+    tiles = NLON // 128
+
+    def strips(ref, r):
+        whole = ref[pl.ds(r, 8), :]
+        return [whole[:, 128 * v : 128 * (v + 1)] for v in range(tiles)]
 
     def row_above(before, x):
         return pltpu.roll(jnp.where(sublane == 7, before, x), 1, 0)
@@ -257,57 +283,79 @@
     def row_below(x, behind):
         return pltpu.roll(jnp.where(sublane == 0, behind, x), 7, 0)
 
-    def forward_strip(src, r):
-        before, x, behind = near(src, r)
-        above = row_above(before, x)
-        below = row_below(x, behind)
-        east = pltpu.roll(x, NLON - 1, 1)
-        west = pltpu.roll(x, 1, 1)
-        return (
-            DIFFUSION * ((x + (east + west)) + (above + below))
-            + half_e[pl.ds(r, 8), :] * (west - east)
-            + half_n[pl.ds(r, 8), :] * (above - below)
-        )
-
-    def adjoint_strip(src, r):
-        before, y, behind = near(src, r)
-        n_before, n, n_behind = near(half_n, r)
-        fifth = DIFFUSION * y
-        zonal = half_e[pl.ds(r, 8), :] * y
-        merid = n * y
-        north = row_above((DIFFUSION - n_before) * before, fifth - merid)
-        south = row_below(fifth + merid, (DIFFUSION + n_behind) * behind)
-        return (
-            (fifth + (north + south))
-            + (pltpu.roll(fifth - zonal, 1, 1) + pltpu.roll(fifth + zonal, NLON - 1, 1))
-        )
+    def forward_strip(src, dst, r):
+        before, x, behind = strips(src, r - 8), strips(src, r), strips(src, r + 8)
+        he, hn = strips(half_e, r), strips(half_n, r)
+        right = [None] * tiles
+        left = [None] * tiles
+        out = []
+        for v in range(tiles):
+            for w in (v - 1, v, v + 1):
+                w = w % tiles
+                if right[w] is None:
+                    right[w], left[w] = pltpu.roll(x[w], 1, 1), pltpu.roll(x[w], 127, 1)
+            above = row_above(before[v], x[v])
+            below = row_below(x[v], behind[v])
+            east = jnp.where(lane == 127, left[(v + 1) % tiles], left[v])
+            west = jnp.where(lane == 0, right[v - 1], right[v])
+            out.append(
+                DIFFUSION * ((x[v] + (east + west)) + (above + below))
+                + he[v] * (west - east)
+                + hn[v] * (above - below)
+            )
+        dst[pl.ds(r, 8), :] = jnp.concatenate(out, axis=1)
+
+    def adjoint_strip(src, dst, r):
+        before, y, behind = strips(src, r - 8), strips(src, r), strips(src, r + 8)
+        n_before, hn, n_behind = strips(half_n, r - 8), strips(half_n, r), strips(half_n, r + 8)
+        he = strips(half_e, r)
+        fifth = [None] * tiles
+        right = [None] * tiles
+        left = [None] * tiles
+        out = []
+        for v in range(tiles):
+            for w in (v - 1, v, v + 1):
+                w = w % tiles
+                if right[w] is None:
+                    fifth[w] = DIFFUSION * y[w]
+                    zonal = he[w] * y[w]
+                    right[w] = pltpu.roll(fifth[w] - zonal, 1, 1)
+                    left[w] = pltpu.roll(fifth[w] + zonal, 127, 1)
+            merid = hn[v] * y[v]
+            north = row_above((DIFFUSION - n_before[v]) * before[v], fifth[v] - merid)
+            south = row_below(fifth[v] + merid, (DIFFUSION + n_behind[v]) * behind[v])
+            east = jnp.where(lane == 127, left[(v + 1) % tiles], left[v])
+            west = jnp.where(lane == 0, right[v - 1], right[v])
+            out.append(fifth[v] + (north + south) + (east + west))
+        dst[pl.ds(r, 8), :] = jnp.concatenate(out, axis=1)
 
     def steps(strip):
         for step in range(STEPS):
-            src, dst = state.at[step % 2], state.at[(step + 1) % 2]
+            src, dst = (state, state_b) if step % 2 == 0 else (state_b, state)
             whole = step < STEPS - 1
 
             def one(i, _):
                 r = pl.multiple_of(8 * i + (TOP - 8 if whole else TOP), 8)
-                dst[pl.ds(r, 8), :] = strip(src, r)
+                strip(src, dst, r)
                 return 0
 
-            lax.fori_loop(0, ROWS // 8 + (2 if whole else 0), one, 0)
+            count = ROWS // 8 + (2 if whole else 0)
+            lax.fori_loop(0, count, one, 0, unroll=count // 2)
             if whole:
                 for side in range(2):
                     at = pl.ds(halo_at[side], 8)
                     dst[at, :] = jnp.where(inside[side], dst[at, :], 0.0)
 
     for at in (TOP - 16, TOP + ROWS + 8):
-        for ref in (state.at[0], state.at[1], half_n):
+        for ref in (state, state_b, half_n):
             ref[pl.ds(at, 8), :] = jnp.zeros((8, NLON), F32)
     steps(adjoint_strip)
-    adj_s[...] = state[0, TOP : TOP + ROWS, :].astype(BF16)
-    adj_copy = pltpu.make_async_remote_copy(
-        src_ref=adj_s, dst_ref=adj_r, send_sem=adj_ss, recv_sem=adj_rs,
-        device_id=(before, me), device_id_type=MESH,
-    )
-    adj_copy.start()
+    adj_s[...] = state[TOP : TOP + ROWS, :].astype(BF16)
+
+    @pl.when(has_previous)
+    def _():
+        adj_copies[0].start()
+
 
     loads["var"].wait()
     varf[:, 0:OWN] = var_v[...].astype(F32).T
@@ -375,20 +423,27 @@
         a2_copy(12 + other, 4 * band + other).start()
     recv2[me] = send2[12 + seat]
 
-    inc_copy.wait_recv()
-    for side in range(2):
-        edge_copies[2 * side + 1].wait_recv()
-    state[0, TOP : TOP + ROWS, :] = inc_r[...].astype(F32)
+    @pl.when(has_previous)
+    def _():
+        adj_copies[1].start()
+
+
+    @pl.when(has_previous)
+    def _():
+        for copy in (*inc_copies, edge_copies[1], edge_copies[3]):
+            copy.wait_recv()
+
+    @pl.when(jnp.logical_not(has_previous))
+    def _():
+        inc_r[...] = jnp.zeros_like(inc_r)
+        inc_edge_r[...] = jnp.zeros_like(inc_edge_r)
+
+    state[TOP : TOP + ROWS, :] = inc_r[...].astype(F32)
     for side in range(2):
         rows = inc_edge_r[side].astype(F32)
         rows = jnp.concatenate([rows[STEPS * q : STEPS * (q + 1)] for q in range(4)], axis=1)
-        state[0, pl.ds(halo_at[side], 8), :] = jnp.where(inside[side], outside(side, rows), 0.0)
+        state[pl.ds(halo_at[side], 8), :] = jnp.where(inside[side], outside(side, rows), 0.0)
     steps(forward_strip)
-
-    adj_copy.wait_recv()
-    kept = jnp.where(tm < windows - 1, 1.0, 0.0)
-    out2_v[...] = (mult_v[...].astype(F32) - kept * adj_r[...].astype(F32)).astype(BF16)
-    out2_copy = load(out2_v, out2_h, out_sem.at[0])
 
     for source in range(SPACE):
 
@@ -415,23 +470,40 @@
             at = SPACE * MAIN + 128 * q
             grid[16 * g : 16 * (g + 1), at : at + 128] = rows.astype(BF16)
 
-    taken = jnp.where(tm > 0, 1.0, 0.0)
-
     def out_step(n, _):
         pltpu.make_async_copy(loni_h.at[n], loni_v.at[n], loni_sem.at[n]).wait()
         at = pl.ds(pl.multiple_of(n * CHUNK, CHUNK), CHUNK)
         term = jnp.dot(grid[...], loni_v[n], preferred_element_type=F32)
-        ahead = state[0, TOP : TOP + ROWS, at]
-        out1_v[:, at] = (term + inc_v[:, at].astype(F32) - taken * ahead).astype(BF16)
+        ahead = state[TOP : TOP + ROWS, at]
+        out1_v[:, at] = term + inc_v[:, at].astype(F32) - ahead
+        pltpu.make_async_copy(out1_v.at[:, at], out1_h.at[:, at], out1_sem.at[n]).start()
         return 0
 
     lax.fori_loop(0, CHUNKS, out_step, 0)
-    out1_copy = load(out1_v, out1_h, out_sem.at[1])
-
-    inc_copy.wait_send()
-    for copy in edge_copies:
+    @pl.when(has_next)
+    def _():
+        for copy in adj_copies:
+            copy.wait_recv()
+
+    @pl.when(jnp.logical_not(has_next))
+    def _():
+        adj_r[...] = jnp.zeros_like(adj_r)
+
+    out2_copy = load(adj_r, out2_h, load_sem.at[7])
+
+    for copy in (edge_copies[0], edge_copies[2]):
         copy.wait_send()
-    adj_copy.wait_send()
+
+    @pl.when(has_next)
+    def _():
+        for copy in (*inc_copies, edge_copies[1], edge_copies[3]):
+            copy.wait_send()
+
+    @pl.when(has_previous)
+    def _():
+        for copy in adj_copies:
+            copy.wait_send()
+
 
     def sent(slot, _):
         for src, dst, ss, rs in ((send1, recv1, a1_ss, a1_rs), (send2, recv2, a2_ss, a2_rs)):
@@ -449,7 +521,13 @@
 
     lax.fori_loop(0, SPACE, sent, 0)
     out2_copy.wait()
-    out1_copy.wait()
+
+    def written(n, _):
+        at = pl.ds(pl.multiple_of(n * CHUNK, CHUNK), CHUNK)
+        pltpu.make_async_copy(out1_v.at[:, at], out1_h.at[:, at], out1_sem.at[n]).wait()
+        return 0
+
+    lax.fori_loop(0, CHUNKS, written, 0)
 
 
 def shards(windows, multiplier, increment, wind_east, wind_north, variances):
@@ -460,7 +538,7 @@
     vmem = pltpu.VMEM
     first, last = pl.pallas_call(
         functools.partial(kernel, windows),
-        out_shape=(jax.ShapeDtypeStruct(block, BF16), jax.ShapeDtypeStruct(block, BF16)),
+        out_shape=(jax.ShapeDtypeStruct(block, F32), jax.ShapeDtypeStruct(block, BF16)),
         in_specs=[pl.BlockSpec(memory_space=pl.ANY)] * 9,
         out_specs=(pl.BlockSpec(memory_space=pl.ANY),) * 2,
         scratch_shapes=[
@@ -471,13 +549,13 @@
             vmem(block, BF16), vmem((2, 16, 640), BF16), vmem((2, 16, 640), BF16),
             vmem((2, 16, NLON), BF16), vmem((2, 16, NLON), BF16),
             vmem(block, BF16), vmem(block, BF16),
-            vmem((2, *wide), F32), vmem(wide, F32), vmem(wide, F32),
+            vmem(wide, F32), vmem(wide, F32), vmem(wide, F32), vmem(wide, F32),
             vmem((SPACE, MSG, 128), BF16), vmem((SPACE, MSG, 128), BF16),
             vmem((SPACE, MSG, 128), BF16), vmem((SPACE, MSG, 128), BF16),
             vmem((NLAT, CHUNK), BF16), vmem((NLAT, CHUNK), BF16), vmem(block, BF16),
-            vmem((NLAT, CHUNK), F32), vmem(block, BF16), vmem(block, BF16),
-            dma((7,)), dma((CHUNKS,)), dma((CHUNKS,)), dma((2,)),
-            dma, dma, dma((2,)), dma((2,)), dma((2,)), dma((2,)), dma, dma,
+            vmem((NLAT, CHUNK), F32), vmem(block, F32),
+            dma((8,)), dma((CHUNKS,)), dma((CHUNKS,)), dma((CHUNKS,)),
+            dma((4,)), dma((2,)), dma((2,)), dma((2,)), dma((2,)), dma((4,)),
             dma((SPACE,)), dma((SPACE,)), dma((SPACE,)), dma((SPACE,)),
         ],
         compiler_params=pltpu.CompilerParams(
@@ -490,7 +568,8 @@
         multiplier[0], increment[0], wind_east[0], wind_north[0],
         jnp.swapaxes(variances[0], 0, 1), lonf, loni, lat, latt,
     )
-    return first[None], last[None]
+    last = (multiplier[0].astype(F32) - last.astype(F32)).astype(BF16)
+    return first.astype(BF16)[None], last[None]
 
 
 def solution(mesh):

time: 62.3 us -> 54.3 us (0.87)
  Pallas kernels: 57.9 us -> 51.3 us
  local copies, waits for them, and re-layouts: 3.56 us -> 0.01 us
  other arithmetic: 0 us -> 2.27 us
    pallas_call x1, Pallas kernels: 57.9 us -> 51.3 us  [shards(): pl.pallas_call(functools.partial(kernel, windows), out_shape=(jax.ShapeDt...]
    unnamed x2, local copies, waits for them, and re-layouts: 3.56 us -> 0.01 us
    broadcast_in_dim x0 -> x1, other arithmetic: none -> 2.27 us  [shards(): return (first.astype(BF16)[None], last[None])]
where the time goes in v1:
time: 54.3 us; the launch traced here: 54.2 us
  Pallas kernels  51.3 us (94%)
  other arithmetic  2.27 us (4%)
  between operations  0.65 us (1%)
    pallas_call x1, Pallas kernels, shards(): pl.pallas_call(functools.partial(kernel, windows), out_shape=(jax.ShapeDt...  51.3 us
    broadcast_in_dim x1, other arithmetic, shards(): return (first.astype(BF16)[None], last[None])  2.27 us

profile of v1, /device:TPU:1, one launch (start us, length us, event | category | flops | bytes accessed | tf_op | source)
XLA Modules:
  0.0 54.2 jit_solution(7708790068601770456)
XLA Ops:
  0.6 0.0 copy-start
  0.6 51.3 %shard_map.104 = (f32[80,2560]{1,0:T(8,128)}, bf16[80,2560]{1,0:T(8,128)(2,1)}) custom-call(bf16[80,2560]{1,0:T(8,128)(2,1)} %bitcast.12, bf16[80,2560]{1,0:T(8,128)(2,1)} %bitcast.13, bf16[80,2560]{1,0:T(8,128)(2,1)} %bitcast.14, bf16[80,2560]{1,0:T(8,128)(2,1)} %bitcast.15, bf16[160,1280]{1,0:T(8,128)(2,1)} %bitcast.16, ...), custom_call_target="tpu_custom_call" | custom-call | flops 3145728000 | bytes 36000000 | tf_op jit(solution)/shard_map/pallas_call | solution.py:539
  51.9 0.0 copy-done
  51.9 2.3 %fusion = (bf16[1,80,2560]{2,1,0:T(8,128)(2,1)}, bf16[1,80,2560]{2,1,0:T(8,128)(2,1)}) fusion(bf16[80,2560]{1,0:T(8,128)(2,1)} %get-tuple-element.5, bf16[1,80,2560]{2,1,0:T(8,128)(2,1)S(1)} %copy-done, f32[80,2560]{1,0:T(8,128)} %get-tuple-element.4), kind=kLoop, calls=%fused_computation.1 | loop fusion | flops 1024000 | bytes 2457600 | tf_op jit(solution)/shard_map/broadcast_in_dim | solution.py:572
Async XLA Ops:
  0.6 51.3 %copy-start = (bf16[1,80,2560]{2,1,0:T(8,128)(2,1)S(1)}, bf16[1,80,2560]{2,1,0:T(8,128)(2,1)}, u32[]{:S(2)}) copy-start(bf16[1,80,2560]{2,1,0:T(8,128)(2,1)} %param.9) | copy-start | bytes 1228804

commit v2 on v1

--- a/solution.py
+++ b/solution.py
@@ -144,6 +144,12 @@
         which = lax.rem(chip + 1 + j, 8)
         lonf_loads.append(load(lonf_h.at[which], lonf_v.at[j], lonf_sem.at[j]))
 
+    loads["var"] = load(var_h, var_v, load_sem.at[4])
+    lat_load = load(lat_h, lat_v, load_sem.at[5])
+    latt_load = load(latt_h, latt_v, load_sem.at[6])
+    for n in range(CHUNKS):
+        load(loni_h.at[n], loni_v.at[n], loni_sem.at[n])
+
     pl.semaphore_wait(barrier, 21)
 
     def exchange(src, dst, sem, to, cut):
@@ -156,7 +162,7 @@
             for n, rows in enumerate((pl.ds(0, cut), pl.ds(cut, ROWS - cut)))
         ]
 
-    inc_copies = exchange(inc_h, inc_r, inc_sem, after, INC_CUT)
+    inc_copies = exchange(inc_v, inc_r, inc_sem, after, INC_CUT)
     adj_copies = exchange(adj_s, adj_r, adj_sem, before, ADJ_CUT)
     has_next, has_previous = tm < windows - 1, tm > 0
 
@@ -235,11 +241,6 @@
         return 0
 
     lax.fori_loop(0, 8, lon_step, 0)
-    loads["var"] = load(var_h, var_v, load_sem.at[4])
-    lat_load = load(lat_h, lat_v, load_sem.at[5])
-    latt_load = load(latt_h, latt_v, load_sem.at[6])
-    for n in range(CHUNKS):
-        load(loni_h.at[n], loni_v.at[n], loni_sem.at[n])
     a1_copy(14 + 1 - core, sibling).start()
     recv1[me] = send1[14 + core]
 

time: 54.3 us -> 54.4 us (level)
  no operation moved by 1% of the time
where the time goes in v2:
time: 54.4 us; the launch traced here: 54.3 us
  Pallas kernels  51.3 us (94%)
  other arithmetic  2.27 us (4%)
  between operations  0.65 us (1%)
    pallas_call x1, Pallas kernels, shards(): pl.pallas_call(functools.partial(kernel, windows), out_shape=(jax.ShapeDt...  51.3 us
    broadcast_in_dim x1, other arithmetic, shards(): return (first.astype(BF16)[None], last[None])  2.27 us

profile of v2, /device:TPU:1, one launch (start us, length us, event | category | flops | bytes accessed | tf_op | source)
XLA Modules:
  0.0 54.3 jit_solution(15859625813092157376)
XLA Ops:
  0.6 0.0 copy-start
  0.6 51.3 %shard_map.104 = (f32[80,2560]{1,0:T(8,128)}, bf16[80,2560]{1,0:T(8,128)(2,1)}) custom-call(bf16[80,2560]{1,0:T(8,128)(2,1)} %bitcast.12, bf16[80,2560]{1,0:T(8,128)(2,1)} %bitcast.13, bf16[80,2560]{1,0:T(8,128)(2,1)} %bitcast.14, bf16[80,2560]{1,0:T(8,128)(2,1)} %bitcast.15, bf16[160,1280]{1,0:T(8,128)(2,1)} %bitcast.16, ...), custom_call_target="tpu_custom_call" | custom-call | flops 3145728000 | bytes 36000000 | tf_op jit(solution)/shard_map/pallas_call | solution.py:540
  52.0 0.0 copy-done
  52.0 2.3 %fusion = (bf16[1,80,2560]{2,1,0:T(8,128)(2,1)}, bf16[1,80,2560]{2,1,0:T(8,128)(2,1)}) fusion(bf16[80,2560]{1,0:T(8,128)(2,1)} %get-tuple-element.5, bf16[1,80,2560]{2,1,0:T(8,128)(2,1)S(1)} %copy-done, f32[80,2560]{1,0:T(8,128)} %get-tuple-element.4), kind=kLoop, calls=%fused_computation.1 | loop fusion | flops 1024000 | bytes 2457600 | tf_op jit(solution)/shard_map/broadcast_in_dim | solution.py:573
Async XLA Ops:
  0.6 51.3 %copy-start = (bf16[1,80,2560]{2,1,0:T(8,128)(2,1)S(1)}, bf16[1,80,2560]{2,1,0:T(8,128)(2,1)}, u32[]{:S(2)}) copy-start(bf16[1,80,2560]{2,1,0:T(8,128)(2,1)} %param.9) | copy-start | bytes 1228804
